TPU v7x, 32 devices: a whole 2x2x4 slice. The times are simulated.
32 devices in a mesh: expert: 16 (over z, y, core), hidden: 2 (over x).
Axes of the slice: x: 2, y: 2, z: 4, core: 2. Of those that a mesh axis runs over, the one named last changes fastest.
Arguments:
- tokens: bfloat16 [4096, 2048], P('expert'), may hold values from -6 to 6
- gates: float32 [4096, 2], P('expert'), may hold values from 0.2 to 1
- routes: int32 [4096, 2], P('expert'), may hold values from 0 to 15, all different within a row; in each aligned block of 256 rows (0 to 255, 256 to 511, ...) at most 48 rows name the same one
- w_up: bfloat16 [16, 2048, 4096], P('expert', None, 'hidden'), may hold values from -0.125 to 0.125
- w_down: bfloat16 [16, 4096, 2048], P('expert', 'hidden'), may hold values from -0.09375 to 0.09375
- cotangent: bfloat16 [4096, 2048], P('expert', 'hidden'), may hold values from -6 to 6
Outputs:
- mixed: bfloat16 [4096, 2048], P('expert', 'hidden')
- grad_tokens: bfloat16 [4096, 2048], P('expert', 'hidden')
- grad_up: bfloat16 [16, 2048, 4096], P('expert', None, 'hidden')
- grad_down: bfloat16 [16, 4096, 2048], P('expert', 'hidden')
Inputs may be any that keep to these rules, and one draw needn't show every extreme that they name: `routes`: each row names 2 different experts. Within each aligned block of 256 rows no expert is named by more than 48 rows, a bound that some block reaches.
All inputs are finite; a program needn't handle non-finite values.
Results may differ from a plain program's by a relative error of at most 0.009.
Values may be sent and summed in bfloat16 or wider, within the bound.
A program may use at most 128 MiB of HBM per device.

v0:
```python
import jax
import jax.numpy as jnp
from jax import lax
from jax.sharding import PartitionSpec as P


def gelu_fn(values):
    return jax.nn.gelu(values, approximate=True)


def gated_slots(selectors, gates, cot_float):
    buffer = jnp.zeros((selectors[0].shape[0], cot_float.shape[1]), jnp.float32)
    for which in range(len(selectors)):
        weighted = (gates[:, which : which + 1] * cot_float).astype(jnp.bfloat16)
        buffer = buffer + jnp.dot(selectors[which], weighted, preferred_element_type=jnp.float32)
    return buffer.astype(jnp.bfloat16)


def per_device(tokens, gates, routes, w_up, w_down, cotangent):
    expert_count = lax.axis_size("expert")
    tok_rows, top_count = routes.shape
    capacity = 3 * tok_rows * top_count // (2 * expert_count)
    slot_total = expert_count * capacity
    flat_routes = routes.reshape(-1)
    member = (flat_routes[:, None] == jnp.arange(expert_count, dtype=jnp.int32)[None, :]).astype(
        jnp.int32
    )
    before = jnp.cumsum(member, axis=0) - member
    slot_place = jnp.sum(before * member, axis=1)
    target = (flat_routes * capacity + slot_place).reshape(tok_rows, top_count)
    slot_ids = jnp.arange(slot_total, dtype=jnp.int32)
    selectors = [
        (target[:, which][None, :] == slot_ids[:, None]).astype(jnp.bfloat16)
        for which in range(top_count)
    ]
    select_all = selectors[0]
    which = 1
    select_all = select_all + selectors[which]
    up_local = w_up[0]
    down_local = w_down[0]
    send_rows = jnp.dot(select_all, tokens, preferred_element_type=jnp.float32).astype(jnp.bfloat16)
    expert_in = lax.all_to_all(send_rows, "expert", split_axis=0, concat_axis=0, tiled=True)
    pre_act = jnp.dot(expert_in, up_local, preferred_element_type=jnp.float32)
    activated, gelu_back = jax.vjp(gelu_fn, pre_act)
    hidden_act = activated.astype(jnp.bfloat16)
    partial_value = jnp.dot(hidden_act, down_local, preferred_element_type=jnp.float32)
    slot_sums = lax.psum_scatter(
        partial_value.astype(jnp.bfloat16), "hidden", scatter_dimension=1, tiled=True
    ).astype(jnp.float32)
    returned = lax.all_to_all(
        slot_sums.astype(jnp.bfloat16), "expert", split_axis=0, concat_axis=0, tiled=True
    ).astype(slot_sums.dtype)
    mixed = gates[:, 0:1] * jnp.take(returned, target[:, 0], axis=0)
    which = 1
    mixed = mixed + gates[:, which : which + 1] * jnp.take(returned, target[:, which], axis=0)
    mixed = mixed.astype(jnp.bfloat16)
    cot_full = lax.all_gather(cotangent, "hidden", axis=1, tiled=True).astype(jnp.float32)
    grad_out = lax.all_to_all(
        gated_slots(selectors, gates, cot_full), "expert", split_axis=0, concat_axis=0, tiled=True
    )
    grad_hidden = lax.dot_general(
        grad_out, down_local, (((1,), (1,)), ((), ())), preferred_element_type=jnp.float32
    )
    grad_pre = gelu_back(grad_hidden)[0].astype(jnp.bfloat16)
    grad_down = lax.dot_general(
        hidden_act, grad_out, (((0,), (0,)), ((), ())), preferred_element_type=jnp.float32
    ).astype(jnp.bfloat16)
    grad_up = lax.dot_general(
        expert_in, grad_pre, (((0,), (0,)), ((), ())), preferred_element_type=jnp.float32
    ).astype(jnp.bfloat16)
    grad_inputs = lax.dot_general(
        grad_pre, up_local, (((1,), (1,)), ((), ())), preferred_element_type=jnp.float32
    )
    input_sums = lax.psum_scatter(
        grad_inputs.astype(jnp.bfloat16), "hidden", scatter_dimension=1, tiled=True
    ).astype(jnp.float32)
    input_back = lax.all_to_all(
        input_sums.astype(jnp.bfloat16), "expert", split_axis=0, concat_axis=0, tiled=True
    ).astype(input_sums.dtype)
    grad_tokens = jnp.take(input_back, target[:, 0], axis=0)
    which = 1
    grad_tokens = grad_tokens + jnp.take(input_back, target[:, which], axis=0)
    grad_tokens = grad_tokens.astype(jnp.bfloat16)
    return (mixed, grad_tokens, grad_up[None], grad_down[None])


def solution(mesh):
    placed = (
        P("expert", None),
        P("expert", None),
        P("expert", None),
        P("expert", None, "hidden"),
        P("expert", "hidden", None),
        P("expert", "hidden"),
    )
    return jax.shard_map(
        per_device,
        mesh=mesh,
        in_specs=placed,
        out_specs=(
            P("expert", "hidden"),
            P("expert", "hidden"),
            P("expert", None, "hidden"),
            P("expert", "hidden", None),
        ),
        check_vma=False,
    )
```

profile of v0, /device:TPU:15, one launch (start us, length us, event | category | flops | bytes accessed | tf_op | source)
XLA Modules:
  0.0 297.4 jit_solution(17705065419141653931)
XLA Ops:
  7.2 0.9 copy.20
  8.4 1.2 reduce-window.6
  10.1 0.7 multiply_add_fusion
  10.8 2.7 convolution_convert_fusion
  13.5 6.6 %all-to-all-start = ((bf16[16,48,2048]{2,1,0:T(8,128)(2,1)}), bf16[16,48,2048]{2,1,0:T(8,128)(2,1)}, u32[]{:S(2)}, u32[]{:S(2)}) async-start(bf16[16,48,2048]{2,1,0:T(8,128)(2,1)} %bitcast.62), calls=%async_computation | async-start | bytes 6291456 | tf_op jit(solution)/shard_map/all_to_all | solution.py:42
  20.1 0.7 all-gather.2.cloned.1.call-update
  20.8 22.6 %all-gather.2.cloned.1.call-done = bf16[256,2048]{1,0:T(8,128)(2,1)} async-done(((bf16[256,1024]{1,0:T(8,128)(2,1)}), bf16[256,2048]{1,0:T(8,128)(2,1)}) %all-gather.2.cloned.1.call-update) | async-done | bytes 1048592 | tf_op jit(solution)/shard_map/all_gather | solution.py:57
  43.4 2.4 fusion.26
  45.8 2.8 add_convert_fusion
  48.6 41.5 %all-to-all-done = bf16[16,48,2048]{2,1,0:T(8,128)(2,1)} async-done(((bf16[16,48,2048]{2,1,0:T(8,128)(2,1)}), bf16[16,48,2048]{2,1,0:T(8,128)(2,1)}, u32[]{:S(2)}, u32[]{:S(2)}) %all-to-all-start) | async-done | bytes 3145760 | tf_op jit(solution)/shard_map/all_to_all | solution.py:42
  90.1 4.9 %all-to-all-start.2 = ((bf16[16,48,2048]{2,1,0:T(8,128)(2,1)}), bf16[16,48,2048]{2,1,0:T(8,128)(2,1)}, u32[]{:S(2)}, u32[]{:S(2)}) async-start(bf16[16,48,2048]{2,1,0:T(8,128)(2,1)} %bitcast.63), calls=%async_computation.3 | async-start | bytes 6291456 | tf_op jit(solution)/shard_map/all_to_all | solution.py:58
  95.0 10.0 %fusion.6 = f32[768,2048]{1,0:T(8,128)S(1)} fusion(bf16[768,2048]{1,0:T(8,128)(2,1)} %bitcast.5, bf16[1,2048,2048]{2,1,0:T(8,128)(2,1)} %param.11), kind=kOutput, calls=%fused_computation.12 | convolution fusion | flops 6442450944 | bytes 17825792 | tf_op jit(solution)/shard_map/dot_general | solution.py:43
  105.1 2.7 copy-done.4
  107.7 11.2 %fusion.18 = bf16[768,2048]{1,0:T(8,128)(2,1)} fusion(bf16[1,2048,2048]{2,1,0:T(8,128)(2,1)} %param.12, f32[768,2048]{1,0:T(8,128)S(1)} %fusion.6), kind=kOutput, calls=%fused_computation.27 | convolution fusion | flops 6458179584 | bytes 17825792 | tf_op jit(solution)/shard_map/dot_general | solution.py:46
  119.0 0.2 reduce-scatter.5.cloned.1.call-start
  119.2 45.7 %all-to-all-done.2 = bf16[16,48,2048]{2,1,0:T(8,128)(2,1)} async-done(((bf16[16,48,2048]{2,1,0:T(8,128)(2,1)}), bf16[16,48,2048]{2,1,0:T(8,128)(2,1)}, u32[]{:S(2)}, u32[]{:S(2)}) %all-to-all-start.2) | async-done | bytes 3145760 | tf_op jit(solution)/shard_map/all_to_all | solution.py:58
  165.0 14.2 %fusion.14 = bf16[768,2048]{1,0:T(8,128)(2,1)S(1)} fusion(f32[768,2048]{1,0:T(8,128)} %copy-done.4, bf16[768,2048]{1,0:T(8,128)(2,1)} %bitcast.13, bf16[1,2048,2048]{2,1,0:T(8,128)(2,1)} %param.12), kind=kOutput, calls=%fused_computation.22 | convolution fusion | flops 6473908224 | bytes 20971520 | tf_op jit(solution)/shard_map/dot_general | solution.py:61
  179.2 1.6 copy-done.5
  180.8 10.2 %fusion.15 = bf16[768,2048]{1,0:T(8,128)(2,1)} fusion(bf16[768,2048]{1,0:T(8,128)(2,1)S(1)} %fusion.14, bf16[1,2048,2048]{2,1,0:T(8,128)(2,1)} %param.11), kind=kOutput, calls=%fused_computation.26 | convolution fusion | flops 6444023808 | bytes 14680064 | tf_op jit(solution)/shard_map/dot_general | solution.py:71
  191.1 4.9 %all-to-all-start.1 = ((bf16[16,48,1024]{2,1,0:T(8,128)(2,1)}), bf16[16,48,1024]{2,1,0:T(8,128)(2,1)S(1)}, u32[]{:S(2)}, u32[]{:S(2)}) async-start(bf16[16,48,1024]{2,1,0:T(8,128)(2,1)} %bitcast.65), calls=%async_computation.2 | async-start | bytes 3145728 | tf_op jit(solution)/shard_map/all_to_all | solution.py:50
  196.1 37.0 %reduce-scatter.5.cloned.1.call-done = bf16[768,1024]{1,0:T(8,128)(2,1)} async-done(((bf16[768,2048]{1,0:T(8,128)(2,1)}), bf16[768,1024]{1,0:T(8,128)(2,1)}) %reduce-scatter.5.cloned.1.call-update) | async-done | bytes 1572880 | tf_op jit(solution)/shard_map/reduce_scatter | solution.py:74
  233.1 6.4 %all-to-all-start.3 = ((bf16[16,48,1024]{2,1,0:T(8,128)(2,1)}), bf16[16,48,1024]{2,1,0:T(8,128)(2,1)}, u32[]{:S(2)}, u32[]{:S(2)}) async-start(bf16[16,48,1024]{2,1,0:T(8,128)(2,1)} %bitcast.64), calls=%async_computation.5 | async-start | bytes 3145728 | tf_op jit(solution)/shard_map/all_to_all | solution.py:77
  239.5 11.4 %convert_bitcast_fusion.1 = bf16[1,2048,2048]{2,1,0:T(8,128)(2,1)} fusion(bf16[768,2048]{1,0:T(8,128)(2,1)} %bitcast.5, bf16[768,2048]{1,0:T(8,128)(2,1)} %copy-done.5), kind=kOutput, calls=%fused_computation.15 | convolution fusion | flops 6446645248 | bytes 14680064 | tf_op jit(solution)/shard_map/dot_general | solution.py:68
  250.8 12.3 %convert_bitcast_fusion = bf16[1,2048,2048]{2,1,0:T(8,128)(2,1)} fusion(bf16[768,2048]{1,0:T(8,128)(2,1)} %bitcast.13, f32[768,2048]{1,0:T(8,128)} %copy-done.4), kind=kOutput, calls=%fused_computation.14 | convolution fusion | flops 6460801024 | bytes 17825792 | tf_op jit(solution)/shard_map/dot_general | solution.py:65
  263.2 2.1 bitcast_convert_fusion.1
  265.3 3.5 %gather_fusion = f32[256,1024]{1,0:T(8,128)S(1)} fusion(f32[768,1024]{1,0:T(8,128)} %bitcast_convert_fusion.1, s32[1024]{0:T(1024)S(1)} %pad_clamp_fusion.1), kind=kCustom, calls=%fused_computation.clone | custom fusion | bytes 2098176 | tf_op jit(solution)/shard_map/jit(_take)/gather | solution.py:53
  268.8 3.5 %gather_fusion.1 = f32[256,1024]{1,0:T(8,128)S(1)} fusion(f32[768,1024]{1,0:T(8,128)} %bitcast_convert_fusion.1, s32[1024]{0:T(1024)S(1)} %pad_clamp_fusion), kind=kCustom, calls=%fused_computation.1.clone | custom fusion | bytes 2098176 | tf_op jit(solution)/shard_map/jit(_take)/gather | solution.py:55
  272.2 3.5 %all-to-all-done.3 = bf16[16,48,1024]{2,1,0:T(8,128)(2,1)} async-done(((bf16[16,48,1024]{2,1,0:T(8,128)(2,1)}), bf16[16,48,1024]{2,1,0:T(8,128)(2,1)}, u32[]{:S(2)}, u32[]{:S(2)}) %all-to-all-start.3) | async-done | bytes 1572896 | tf_op jit(solution)/shard_map/all_to_all | solution.py:77
  275.8 3.4 %bitcast_convert_fusion = f32[768,1024]{1,0:T(8,128)} fusion(bf16[16,48,1024]{2,1,0:T(8,128)(2,1)} %all-to-all-done.3), kind=kLoop, calls=%fused_computation.32 | loop fusion | flops 786432 | bytes 4718592 | tf_op jit(solution)/shard_map/convert_element_type | solution.py:79
  279.2 4.5 %gather_fusion.2 = f32[256,1024]{1,0:T(8,128)} fusion(f32[768,1024]{1,0:T(8,128)} %bitcast_convert_fusion, s32[1024]{0:T(1024)S(1)} %pad_clamp_fusion.1), kind=kCustom, calls=%fused_computation.2.clone | custom fusion | bytes 2098176 | tf_op jit(solution)/shard_map/jit(_take)/gather | solution.py:80
  283.7 4.4 %gather_fusion.3 = f32[256,1024]{1,0:T(8,128)} fusion(f32[768,1024]{1,0:T(8,128)} %bitcast_convert_fusion, s32[1024]{0:T(1024)S(1)} %pad_clamp_fusion), kind=kCustom, calls=%fused_computation.3.clone | custom fusion | bytes 2098176 | tf_op jit(solution)/shard_map/jit(_take)/gather | solution.py:82
  288.1 2.8 fusion.28
  (33 shorter events, 1.1 us)
Async XLA Ops:
  7.2 3.7 %copy-start = (bf16[256,2048]{1,0:T(8,128)(2,1)S(1)}, bf16[256,2048]{1,0:T(8,128)(2,1)}, u32[]{:S(2)}) copy-start(bf16[256,2048]{1,0:T(8,128)(2,1)} %param.8) | copy-start | bytes 3145732
  10.8 10.0 %copy-start.3 = (f32[256,2]{0,1:T(2,128)S(1)}, f32[256,2]{0,1:T(2,128)}, u32[]{:S(2)}) copy-start(f32[256,2]{0,1:T(2,128)} %param.9) | copy-start | bytes 6148
  13.5 76.5 %all-to-all-start = ((bf16[16,48,2048]{2,1,0:T(8,128)(2,1)}), bf16[16,48,2048]{2,1,0:T(8,128)(2,1)}, u32[]{:S(2)}, u32[]{:S(2)}) async-start(bf16[16,48,2048]{2,1,0:T(8,128)(2,1)} %bitcast.62), calls=%async_computation | async-start | bytes 6291456 | tf_op jit(solution)/shard_map/all_to_all | solution.py:42
  20.1 23.4 %all-gather.2.cloned.1.call-start = ((), (), s32[]{:S(2)}) async-start(), calls=%async_computation.7 | async-start | bytes 1572864 | tf_op jit(solution)/shard_map/all_gather | solution.py:57
  43.4 2.4 copy-start.2
  90.1 74.9 %all-to-all-start.2 = ((bf16[16,48,2048]{2,1,0:T(8,128)(2,1)}), bf16[16,48,2048]{2,1,0:T(8,128)(2,1)}, u32[]{:S(2)}, u32[]{:S(2)}) async-start(bf16[16,48,2048]{2,1,0:T(8,128)(2,1)} %bitcast.63), calls=%async_computation.3 | async-start | bytes 6291456 | tf_op jit(solution)/shard_map/all_to_all | solution.py:58
  95.0 96.1 %reduce-scatter.3.cloned.1.call-start = ((), (), s32[]{:S(2)}) async-start(), calls=%async_computation.6 | async-start | bytes 4718592 | tf_op jit(solution)/shard_map/reduce_scatter | solution.py:47
  105.0 2.7 copy-start.4
  119.0 114.1 %reduce-scatter.5.cloned.1.call-start = ((), (), s32[]{:S(2)}) async-start(), calls=%async_computation.8 | async-start | bytes 4718592 | tf_op jit(solution)/shard_map/reduce_scatter | solution.py:74
  179.2 1.6 copy-start.5
  191.1 42.0 %all-to-all-start.1 = ((bf16[16,48,1024]{2,1,0:T(8,128)(2,1)}), bf16[16,48,1024]{2,1,0:T(8,128)(2,1)S(1)}, u32[]{:S(2)}, u32[]{:S(2)}) async-start(bf16[16,48,1024]{2,1,0:T(8,128)(2,1)} %bitcast.65), calls=%async_computation.2 | async-start | bytes 3145728 | tf_op jit(solution)/shard_map/all_to_all | solution.py:50
  233.1 42.7 %all-to-all-start.3 = ((bf16[16,48,1024]{2,1,0:T(8,128)(2,1)}), bf16[16,48,1024]{2,1,0:T(8,128)(2,1)}, u32[]{:S(2)}, u32[]{:S(2)}) async-start(bf16[16,48,1024]{2,1,0:T(8,128)(2,1)} %bitcast.64), calls=%async_computation.5 | async-start | bytes 3145728 | tf_op jit(solution)/shard_map/all_to_all | solution.py:77
  279.2 11.7 %copy-start.1 = (bf16[256,2048]{1,0:T(8,128)(2,1)S(1)}, bf16[256,2048]{1,0:T(8,128)(2,1)}, u32[]{:S(2)}) copy-start(bf16[256,2048]{1,0:T(8,128)(2,1)} %param.8) | copy-start | bytes 3145732
Sparse Core Ops, SparseCore 0:
  22.4 20.9 all-gather.1
  119.1 43.0 reduce-scatter.2
  191.2 41.8 reduce-scatter.4
where the time goes:
time: 299 us; the launch traced here: 297 us
  waiting for transfers between devices  151 us (51%)
  matrix products  77.2 us (26%)
  starting transfers between devices  23 us (8%)
  local copies, waits for them, and re-layouts  21.7 us (7%)
  between operations  13.9 us (5%)
  other arithmetic  10.4 us (3%)
    all_to_all x1, waiting for transfers between devices, per_device(): lax.all_to_all(gated_slots(selectors, gates, cot_full), 'expert', split_a...  45.7 us
    all_to_all x1, waiting for transfers between devices, per_device(): lax.all_to_all(send_rows, 'expert', split_axis=0, concat_axis=0, tiled=True)  41.5 us
    reduce_scatter x1, waiting for transfers between devices, per_device(): lax.psum_scatter(grad_inputs.astype(jnp.bfloat16), 'hidden', scatter_dime...  37 us
    all_gather x1, waiting for transfers between devices, per_device(): lax.all_gather(cotangent, 'hidden', axis=1, tiled=True).astype(jnp.float32)  22.6 us
    dot_general x1, matrix products, per_device(): lax.dot_general(grad_out, down_local, (((1,), (1,)), ((), ())), preferred...  14.2 us
    dot_general x1, matrix products, per_device(): lax.dot_general(hidden_act, grad_out, (((0,), (0,)), ((), ())), preferred...  12.3 us
    dot_general x1, matrix products, per_device(): lax.dot_general(expert_in, grad_pre, (((0,), (0,)), ((), ())), preferred_...  11.4 us
    dot_general x1, matrix products, per_device(): jnp.dot(hidden_act, down_local, preferred_element_type=jnp.float32)  11.2 us
  transfers between devices with their start and end apart: 7, of which 5 were waited for; matrix products, arithmetic and copies ran while one was open for 28% of the time, Pallas kernels for 0%

commit v1 on v0

v1 whole, which is shorter than its diff:
```python
import jax
import jax.numpy as jnp
from jax import lax
from jax.sharding import PartitionSpec as P

CHUNKS = 1


def gelu_fn(values):
    return jax.nn.gelu(values, approximate=True)


def swap(block):
    return lax.ppermute(block, "hidden", [(0, 1), (1, 0)])


def gather_features(block):
    if lax.axis_size("hidden") != 2:
        return lax.all_gather(block, "hidden", axis=1, tiled=True)
    other = swap(block)
    first = lax.axis_index("hidden") == 0
    return jnp.concatenate(
        [jnp.where(first, block, other), jnp.where(first, other, block)], axis=1
    )


def summed_features(rows, weight, contract):
    def product(part):
        return lax.dot_general(
            rows, part, (((1,), (contract,)), ((), ())), preferred_element_type=jnp.float32
        ).astype(jnp.bfloat16)

    if lax.axis_size("hidden") != 2:
        return lax.psum_scatter(product(weight), "hidden", scatter_dimension=1, tiled=True)
    axis = 1 - contract
    width = weight.shape[axis] // 2
    me = lax.axis_index("hidden")
    moving = swap(product(lax.dynamic_slice_in_dim(weight, (1 - me) * width, width, axis)))
    kept = product(lax.dynamic_slice_in_dim(weight, me * width, width, axis))
    return (kept.astype(jnp.float32) + moving.astype(jnp.float32)).astype(jnp.bfloat16)


def exchange(block):
    return lax.all_to_all(block, "expert", split_axis=0, concat_axis=0, tiled=True)


def per_device(tokens, gates, routes, w_up, w_down, cotangent):
    expert_count = lax.axis_size("expert")
    tok_rows, top_count = routes.shape
    capacity = 3 * tok_rows * top_count // (2 * expert_count)
    depth = capacity // CHUNKS
    flat_routes = routes.reshape(-1)
    member = (flat_routes[:, None] == jnp.arange(expert_count, dtype=jnp.int32)[None, :]).astype(
        jnp.bfloat16
    )
    order = jnp.arange(tok_rows * top_count, dtype=jnp.int32)
    earlier = (order[:, None] > order[None, :]).astype(jnp.bfloat16)
    before = jnp.dot(earlier, member, preferred_element_type=jnp.float32)
    slot_place = jnp.sum(before * member.astype(jnp.float32), axis=1).astype(jnp.int32)
    slot_chunk = slot_place // depth
    target = (flat_routes * depth + slot_place % depth).reshape(tok_rows, top_count)
    slot_chunk = slot_chunk.reshape(tok_rows, top_count)
    slot_ids = jnp.arange(expert_count * depth, dtype=jnp.int32)

    def selector(chunk, which):
        aim = jnp.where(slot_chunk[:, which] == chunk, target[:, which], -1)
        return (aim[None, :] == slot_ids[:, None]).astype(jnp.bfloat16)

    picks = [[selector(chunk, which) for which in range(top_count)] for chunk in range(CHUNKS)]
    up_local = w_up[0]
    down_local = w_down[0]
    width = cotangent.shape[1]
    own_tokens = lax.dynamic_slice_in_dim(tokens, lax.axis_index("hidden") * width, width, 1)
    cot_float = cotangent.astype(jnp.float32)
    gated = jnp.concatenate(
        [(gates[:, k : k + 1] * cot_float).astype(jnp.bfloat16) for k in range(top_count)], axis=0
    )
    got_tokens = [
        exchange(
            jnp.dot(sum(pick[1:], pick[0]), own_tokens, preferred_element_type=jnp.float32).astype(
                jnp.bfloat16
            )
        )
        for pick in picks
    ]
    got_grads = [
        exchange(
            jnp.dot(
                jnp.concatenate(pick, axis=1), gated, preferred_element_type=jnp.float32
            ).astype(jnp.bfloat16)
        )
        for pick in picks
    ]
    hidden_acts, backs, expert_ins, grad_outs, grad_pres = [], [], [], [], []
    returned, input_back = [], []
    for got in got_tokens:
        expert_in = gather_features(got)
        pre_act = jnp.dot(expert_in, up_local, preferred_element_type=jnp.float32)
        activated, gelu_back = jax.vjp(gelu_fn, pre_act)
        hidden_act = activated.astype(jnp.bfloat16)
        returned.append(exchange(summed_features(hidden_act, down_local, 0)))
        expert_ins.append(expert_in)
        hidden_acts.append(hidden_act)
        backs.append(gelu_back)
    for got, gelu_back in zip(got_grads, backs):
        grad_out = gather_features(got)
        grad_hidden = lax.dot_general(
            grad_out, down_local, (((1,), (1,)), ((), ())), preferred_element_type=jnp.float32
        )
        grad_pre = gelu_back(grad_hidden)[0].astype(jnp.bfloat16)
        input_back.append(exchange(summed_features(grad_pre, up_local, 1)))
        grad_outs.append(grad_out)
        grad_pres.append(grad_pre)

    def outer(left, right):
        return lax.dot_general(
            jnp.concatenate(left, axis=0),
            jnp.concatenate(right, axis=0),
            (((0,), (0,)), ((), ())),
            preferred_element_type=jnp.float32,
        ).astype(jnp.bfloat16)

    grad_down = outer(hidden_acts, grad_outs)
    grad_up = outer(expert_ins, grad_pres)

    def picked(which, arrays):
        total = None
        for pick, array in zip(picks, arrays):
            part = lax.dot_general(
                pick[which], array, (((0,), (0,)), ((), ())), preferred_element_type=jnp.float32
            )
            total = part if total is None else total + part
        return total

    mixed = sum(gates[:, k : k + 1] * picked(k, returned) for k in range(top_count))
    grad_tokens = sum(picked(k, input_back) for k in range(top_count))
    return (
        mixed.astype(jnp.bfloat16),
        grad_tokens.astype(jnp.bfloat16),
        grad_up[None],
        grad_down[None],
    )


def solution(mesh):
    placed = (
        P("expert", None),
        P("expert", None),
        P("expert", None),
        P("expert", None, "hidden"),
        P("expert", "hidden", None),
        P("expert", "hidden"),
    )
    return jax.shard_map(
        per_device,
        mesh=mesh,
        in_specs=placed,
        out_specs=(
            P("expert", "hidden"),
            P("expert", "hidden"),
            P("expert", None, "hidden"),
            P("expert", "hidden", None),
        ),
        check_vma=False,
    )
```

time: 299 us -> 271 us (0.906)
  local copies, waits for them, and re-layouts: 21.7 us -> 1.62 us
  between operations: 13.9 us -> 0.94 us
  matrix products: 77.2 us -> 86.5 us
  other arithmetic: 10.4 us -> 3.69 us
    ppermute x0 -> x4, waiting for transfers between devices: none -> 70.6 us  [swap(): return lax.ppermute(block, 'hidden', [(0, 1), (1, 0)])]
    reduce_scatter x2 -> x0, waiting for transfers between devices: 37 us -> none  [the longest x1 37 us: per_device(): lax.psum_scatter(grad_inputs.astype(jnp.bfloat16), 'hidden', scatter_dime...]
    all_gather x1 -> x0, waiting for transfers between devices: 22.6 us -> none  [per_device(): lax.all_gather(cotangent, 'hidden', axis=1, tiled=True).astype(jnp.float32)]
    gather x4 -> x0, local copies, waits for them, and re-layouts: 15.8 us -> none  [the longest x1 4.47 us: per_device(): grad_tokens = jnp.take(input_back, target[:, 0], axis=0)]
    all_to_all x4, waiting for transfers between devices: 90.7 us -> 82 us  [exchange(): lax.all_to_all(block, 'expert', split_axis=0, concat_axis=0, tiled=True)]
    convert_element_type x4 -> x2, other arithmetic: 8.43 us -> 0.48 us  [the longest x1 0.25 us: selector(): return (aim[None, :] == slot_ids[:, None]).astype(jnp.bfloat16)]
    dot_general x7 -> x13, matrix products: 53 us -> 59.6 us  [the longest x4 26.5 us: product(): lax.dot_general(rows, part, (((1,), (contract,)), ((), ())), preferred_el...]
    unnamed x13 -> x31, local copies, waits for them, and re-layouts: 5.21 us -> 0.88 us
  transfers between devices with their start and end apart: 7 -> 8, of which waited for: 5 -> 6; matrix products, arithmetic and copies ran while one was open for 28% -> 27% of each run, Pallas kernels for 0% -> 0%
where the time goes in v1:
time: 271 us
  waiting for transfers between devices  153 us (56%)
  matrix products  86.5 us (32%)
  starting transfers between devices  25.5 us (9%)
  other arithmetic  3.69 us (1%)
    all_to_all x4, waiting for transfers between devices, exchange(): lax.all_to_all(block, 'expert', split_axis=0, concat_axis=0, tiled=True)  82 us
    ppermute x4, waiting for transfers between devices, swap(): return lax.ppermute(block, 'hidden', [(0, 1), (1, 0)])  70.6 us
    dot_general x4, matrix products, product(): lax.dot_general(rows, part, (((1,), (contract,)), ((), ())), preferred_el...  26.5 us
    all_to_all x4, starting transfers between devices, exchange(): lax.all_to_all(block, 'expert', split_axis=0, concat_axis=0, tiled=True)  23.3 us
    dot_general x2, matrix products, outer(): lax.dot_general(jnp.concatenate(left, axis=0), jnp.concatenate(right, axi...  22 us
    dot_general x1, matrix products, per_device(): lax.dot_general(grad_out, down_local, (((1,), (1,)), ((), ())), preferred...  16.7 us
    dot_general x1, matrix products, per_device(): pre_act = jnp.dot(expert_in, up_local, preferred_element_type=jnp.float32)  10.2 us
    dot_general x4, matrix products, picked(): lax.dot_general(pick[which], array, (((0,), (0,)), ((), ())), preferred_e...  6.9 us
  transfers between devices with their start and end apart: 8, of which 6 were waited for; matrix products, arithmetic and copies ran while one was open for 27% of the time, Pallas kernels for 0%

profile of v1, /device:TPU:15, one launch (start us, length us, event | category | flops | bytes accessed | tf_op | source)
XLA Modules:
  0.0 270.8 jit_solution(1581073791632040119)
XLA Ops:
  0.7 0.8 broadcast_multiply_fusion
  1.5 0.8 copy.13
  2.4 0.3 fusion.44
  3.7 1.7 convolution_convert_fusion.1
  5.4 6.6 %all-to-all-start = ((bf16[16,48,1024]{2,1,0:T(8,128)(2,1)}), bf16[16,48,1024]{2,1,0:T(8,128)(2,1)S(1)}, u32[]{:S(2)}, u32[]{:S(2)}) async-start(bf16[16,48,1024]{2,1,0:T(8,128)(2,1)} %bitcast.1), calls=%async_computation | async-start | bytes 3145728 | tf_op jit(solution)/shard_map/all_to_all | solution.py:44
  12.5 2.1 convolution_convert_fusion
  14.6 33.5 %all-to-all-done = bf16[16,48,1024]{2,1,0:T(8,128)(2,1)S(1)} async-done(((bf16[16,48,1024]{2,1,0:T(8,128)(2,1)}), bf16[16,48,1024]{2,1,0:T(8,128)(2,1)S(1)}, u32[]{:S(2)}, u32[]{:S(2)}) %all-to-all-start) | async-done | bytes 1572896 | tf_op jit(solution)/shard_map/all_to_all | solution.py:44
  48.2 4.9 %all-to-all-start.2 = ((bf16[16,48,1024]{2,1,0:T(8,128)(2,1)}), bf16[16,48,1024]{2,1,0:T(8,128)(2,1)S(1)}, u32[]{:S(2)}, u32[]{:S(2)}) async-start(bf16[16,48,1024]{2,1,0:T(8,128)(2,1)} %bitcast.61), calls=%async_computation.2 | async-start | bytes 3145728 | tf_op jit(solution)/shard_map/all_to_all | solution.py:44
  53.1 0.3 collective-permute-start
  53.4 36.3 %all-to-all-done.2 = bf16[16,48,1024]{2,1,0:T(8,128)(2,1)S(1)} async-done(((bf16[16,48,1024]{2,1,0:T(8,128)(2,1)}), bf16[16,48,1024]{2,1,0:T(8,128)(2,1)S(1)}, u32[]{:S(2)}, u32[]{:S(2)}) %all-to-all-start.2) | async-done | bytes 1572896 | tf_op jit(solution)/shard_map/all_to_all | solution.py:44
  89.9 1.8 broadcast_select_fusion.3
  91.7 10.2 %fusion.2 = f32[768,2048]{1,0:T(8,128)S(1)} fusion(bf16[1,2048,2048]{2,1,0:T(8,128)(2,1)} %param.9, bf16[768,1024]{1,0:T(8,128)(2,1)S(1)} %get-tuple-element.9, bf16[768,1024]{1,0:T(8,128)(2,1)S(1)} %get-tuple-element.8), kind=kOutput, calls=%fused_computation.4 | convolution fusion | flops 6448742400 | bytes 17825792 | tf_op jit(solution)/shard_map/dot_general | solution.py:98
  102.0 3.9 %fusion.28 = bf16[768,1024]{1,0:T(8,128)(2,1)S(1)} fusion(bf16[1,2048,2048]{2,1,0:T(8,128)(2,1)S(1)} %bitcast.69, s32[]{:T(128)S(6)} %select_n.74, f32[768,2048]{1,0:T(8,128)S(1)} %fusion.2), kind=kOutput, calls=%fused_computation.34 | convolution fusion | flops 3236167680 | bytes 12058628 | tf_op jit(solution)/shard_map/dot_general | solution.py:29
  105.9 1.3 collective-permute-start.1
  107.2 18.6 %collective-permute-done.2 = bf16[768,1024]{1,0:T(8,128)(2,1)S(1)} collective-permute-done((bf16[768,1024]{1,0:T(8,128)(2,1)S(1)}, bf16[768,1024]{1,0:T(8,128)(2,1)S(1)}, u32[]{:S(2)}, u32[]{:S(2)}) %collective-permute-start.2) | collective-permute-done | bytes 1572896 | tf_op jit(solution)/shard_map/ppermute | solution.py:14
  125.8 0.3 broadcast_select_fusion.1
  126.1 16.7 %fusion.10 = bf16[768,2048]{1,0:T(8,128)(2,1)} fusion(f32[768,2048]{1,0:T(8,128)} %copy-done.10, bf16[1,2048,2048]{2,1,0:T(8,128)(2,1)} %param.10, bf16[768,1024]{1,0:T(8,128)(2,1)S(1)} %get-tuple-element.7, bf16[768,1024]{1,0:T(8,128)(2,1)S(1)} %get-tuple-element.6), kind=kOutput, calls=%fused_computation.14 | convolution fusion | flops 6480199680 | bytes 20971520 | tf_op jit(solution)/shard_map/dot_general | solution.py:107
  142.8 16.7 %collective-permute-done.1 = bf16[768,1024]{1,0:T(8,128)(2,1)S(1)} collective-permute-done((bf16[768,1024]{1,0:T(8,128)(2,1)S(1)}, bf16[768,1024]{1,0:T(8,128)(2,1)S(1)}, u32[]{:S(2)}, u32[]{:S(2)}) %collective-permute-start.1) | collective-permute-done | bytes 1572896 | tf_op jit(solution)/shard_map/ppermute | solution.py:14
  159.5 9.1 %add_convert_fusion.1 = bf16[768,1024]{1,0:T(8,128)(2,1)} fusion(bf16[768,1024]{1,0:T(8,128)(2,1)S(1)} %collective-permute-done.1, bf16[1,2048,2048]{2,1,0:T(8,128)(2,1)} %param.10, s32[]{:T(128)S(6)} %select_n.71, f32[768,2048]{1,0:T(8,128)} %copy-done.10), kind=kOutput, calls=%fused_computation.31 | convolution fusion | flops 3239313408 | bytes 13631492 | tf_op jit(solution)/shard_map/dot_general | solution.py:29
  168.6 5.0 %all-to-all-start.1 = ((bf16[16,48,1024]{2,1,0:T(8,128)(2,1)}), bf16[16,48,1024]{2,1,0:T(8,128)(2,1)S(1)}, u32[]{:S(2)}, u32[]{:S(2)}) async-start(bf16[16,48,1024]{2,1,0:T(8,128)(2,1)} %bitcast.63), calls=%async_computation.1 | async-start | bytes 3145728 | tf_op jit(solution)/shard_map/all_to_all | solution.py:44
  173.6 6.7 %fusion.34 = bf16[768,1024]{1,0:T(8,128)(2,1)S(1)} fusion(bf16[768,2048]{1,0:T(8,128)(2,1)} %fusion.10, bf16[1,2048,2048]{2,1,0:T(8,128)(2,1)} %param.9, s32[]{:T(128)S(6)} %select_n.74), kind=kOutput, calls=%fused_computation.36 | convolution fusion | flops 3222011904 | bytes 8912900 | tf_op jit(solution)/shard_map/dot_general | solution.py:29
  180.3 0.3 collective-permute-start.3
  180.6 35.4 %collective-permute-done.3 = bf16[768,1024]{1,0:T(8,128)(2,1)S(1)} collective-permute-done((bf16[768,1024]{1,0:T(8,128)(2,1)S(1)}, bf16[768,1024]{1,0:T(8,128)(2,1)S(1)}, u32[]{:S(2)}, u32[]{:S(2)}) %collective-permute-start.3) | collective-permute-done | bytes 1572896 | tf_op jit(solution)/shard_map/ppermute | solution.py:14
  216.0 6.8 %add_convert_fusion = bf16[768,1024]{1,0:T(8,128)(2,1)} fusion(bf16[768,1024]{1,0:T(8,128)(2,1)S(1)} %collective-permute-done.3, bf16[768,2048]{1,0:T(8,128)(2,1)S(1)} %copy-done.11, bf16[1,2048,2048]{2,1,0:T(8,128)(2,1)} %param.9, s32[]{:T(128)S(6)} %select_n.71), kind=kOutput, calls=%fused_computation.30 | convolution fusion | flops 3225157632 | bytes 10485764 | tf_op jit(solution)/shard_map/dot_general | solution.py:29
  222.8 6.9 %all-to-all-start.3 = ((bf16[16,48,1024]{2,1,0:T(8,128)(2,1)}), bf16[16,48,1024]{2,1,0:T(8,128)(2,1)}, u32[]{:S(2)}, u32[]{:S(2)}) async-start(bf16[16,48,1024]{2,1,0:T(8,128)(2,1)} %bitcast.62), calls=%async_computation.3 | async-start | bytes 3145728 | tf_op jit(solution)/shard_map/all_to_all | solution.py:44
  229.7 12.5 %convert_bitcast_fusion = bf16[1,2048,2048]{2,1,0:T(8,128)(2,1)} fusion(bf16[768,1024]{1,0:T(8,128)(2,1)} %copy-done.7, bf16[768,1024]{1,0:T(8,128)(2,1)} %copy-done.6, f32[768,2048]{1,0:T(8,128)} %copy-done.10), kind=kOutput, calls=%fused_computation.6 | convolution fusion | flops 6467092480 | bytes 17825792 | tf_op jit(solution)/shard_map/dot_general | solution.py:116
  242.2 9.5 %convert_bitcast_fusion.1 = bf16[1,2048,2048]{2,1,0:T(8,128)(2,1)} fusion(bf16[768,2048]{1,0:T(8,128)(2,1)S(1)} %copy-done.12, bf16[768,1024]{1,0:T(8,128)(2,1)S(1)} %copy-done.5, bf16[768,1024]{1,0:T(8,128)(2,1)S(1)} %copy-done.3), kind=kOutput, calls=%fused_computation.7 | convolution fusion | flops 6452936704 | bytes 14680064 | tf_op jit(solution)/shard_map/dot_general | solution.py:116
  251.7 0.6 convolution_multiply_fusion.1
  252.3 1.4 fusion.39
  253.8 12.2 %all-to-all-done.3 = bf16[16,48,1024]{2,1,0:T(8,128)(2,1)} async-done(((bf16[16,48,1024]{2,1,0:T(8,128)(2,1)}), bf16[16,48,1024]{2,1,0:T(8,128)(2,1)}, u32[]{:S(2)}, u32[]{:S(2)}) %all-to-all-start.3) | async-done | bytes 1572896 | tf_op jit(solution)/shard_map/all_to_all | solution.py:44
  265.9 2.0 fusion.53
  268.0 2.8 %fusion.38 = bf16[256,1024]{1,0:T(8,128)(2,1)} fusion(f32[256,1024]{1,0:T(8,128)S(1)} %fusion.53, bf16[768,1024]{1,0:T(8,128)(2,1)} %bitcast.15, s32[256]{0:T(256)S(1)} %get-tuple-element.5), kind=kOutput, calls=%fused_computation.48 | convolution fusion | flops 403374080 | bytes 3146752 | tf_op jit(solution)/shard_map/dot_general | solution.py:129
  (46 shorter events, 1.9 us)
Async XLA Ops:
  0.6 3.1 %copy-start = (bf16[256,2048]{1,0:T(8,128)(2,1)S(1)}, bf16[256,2048]{1,0:T(8,128)(2,1)}, u32[]{:S(2)}) copy-start(bf16[256,2048]{1,0:T(8,128)(2,1)} %param.6) | copy-start | bytes 3145732
  0.6 11.3 %copy-start.9 = (f32[256,2]{0,1:T(2,128)S(1)}, f32[256,2]{0,1:T(2,128)}, u32[]{:S(2)}) copy-start(f32[256,2]{0,1:T(2,128)} %param.7) | copy-start | bytes 6148
  0.7 11.6 %copy-start.8 = (bf16[256,1024]{1,0:T(8,128)(2,1)S(1)}, bf16[256,1024]{1,0:T(8,128)(2,1)}, u32[]{:S(2)}) copy-start(bf16[256,1024]{1,0:T(8,128)(2,1)} %param.11) | copy-start | bytes 1572868
  5.4 42.7 %all-to-all-start = ((bf16[16,48,1024]{2,1,0:T(8,128)(2,1)}), bf16[16,48,1024]{2,1,0:T(8,128)(2,1)S(1)}, u32[]{:S(2)}, u32[]{:S(2)}) async-start(bf16[16,48,1024]{2,1,0:T(8,128)(2,1)} %bitcast.1), calls=%async_computation | async-start | bytes 3145728 | tf_op jit(solution)/shard_map/all_to_all | solution.py:44
  48.2 41.5 %all-to-all-start.2 = ((bf16[16,48,1024]{2,1,0:T(8,128)(2,1)}), bf16[16,48,1024]{2,1,0:T(8,128)(2,1)S(1)}, u32[]{:S(2)}, u32[]{:S(2)}) async-start(bf16[16,48,1024]{2,1,0:T(8,128)(2,1)} %bitcast.61), calls=%async_computation.2 | async-start | bytes 3145728 | tf_op jit(solution)/shard_map/all_to_all | solution.py:44
  53.1 36.8 %collective-permute-start = (bf16[768,1024]{1,0:T(8,128)(2,1)S(1)}, bf16[768,1024]{1,0:T(8,128)(2,1)}, u32[]{:S(2)}, u32[]{:S(2)}) collective-permute-start(bf16[768,1024]{1,0:T(8,128)(2,1)S(1)} %bitcast.59), channel_id=1, source_target_pairs={{0,1},{1,0},{2,3},{3,2},{4,5},{5,4},{6,7},{7,6},{8,9},{9,8},{10,11... | collective-permute-start | bytes 4718600 | tf_op jit(solution)/shard_map/ppermute | solution.py:14
  89.7 36.1 %collective-permute-start.2 = (bf16[768,1024]{1,0:T(8,128)(2,1)S(1)}, bf16[768,1024]{1,0:T(8,128)(2,1)S(1)}, u32[]{:S(2)}, u32[]{:S(2)}) collective-permute-start(bf16[768,1024]{1,0:T(8,128)(2,1)S(1)} %bitcast.60), channel_id=1, source_target_pairs={{0,1},{1,0},{2,3},{3,2},{4,5},{5,4},{6,7},{7,6},{8,9},{9,8},{10,11... | collective-permute-start | bytes 4718600 | tf_op jit(solution)/shard_map/ppermute | solution.py:14
  89.9 12.1 %slice-start = ((s8[8388608]{0:T(1024)(128)(4,1)}), s8[4194304]{0:T(1024)(128)(4,1)S(1)}, s32[]{:S(2)}) async-start(s8[8388608]{0:T(1024)(128)(4,1)} %bitcast.68), calls=%async_computation.4 | async-start | bytes 8388608
  91.7 10.3 %copy-start.2 = (bf16[768,1024]{1,0:T(8,128)(2,1)}, bf16[768,1024]{1,0:T(8,128)(2,1)S(1)}, u32[]{:S(2)}) copy-start(bf16[768,1024]{1,0:T(8,128)(2,1)S(1)} %get-tuple-element.8) | copy-start | bytes 4718596
  91.7 10.3 %copy-start.4 = (bf16[768,1024]{1,0:T(8,128)(2,1)}, bf16[768,1024]{1,0:T(8,128)(2,1)S(1)}, u32[]{:S(2)}) copy-start(bf16[768,1024]{1,0:T(8,128)(2,1)S(1)} %get-tuple-element.9) | copy-start | bytes 4718596
  91.7 10.3 %slice-start.1 = ((s8[8388608]{0:T(1024)(128)(4,1)}), s8[4194304]{0:T(1024)(128)(4,1)S(1)}, s32[]{:S(2)}) async-start(s8[8388608]{0:T(1024)(128)(4,1)} %bitcast.68), calls=%async_computation.5 | async-start | bytes 8388608
  102.0 3.9 %copy-start.10 = (f32[768,2048]{1,0:T(8,128)}, f32[768,2048]{1,0:T(8,128)S(1)}, u32[]{:S(2)}) copy-start(f32[768,2048]{1,0:T(8,128)S(1)} %fusion.2) | copy-start | bytes 18874372
  105.9 53.6 %collective-permute-start.1 = (bf16[768,1024]{1,0:T(8,128)(2,1)S(1)}, bf16[768,1024]{1,0:T(8,128)(2,1)S(1)}, u32[]{:S(2)}, u32[]{:S(2)}) collective-permute-start(bf16[768,1024]{1,0:T(8,128)(2,1)S(1)} %fusion.28), channel_id=1, source_target_pairs={{0,1},{1,0},{2,3},{3,2},{4,5},{5,4},{6,7},{7,6},{8,9},{9,8},{10,11... | collective-permute-start | bytes 4718600 | tf_op jit(solution)/shard_map/ppermute | solution.py:14
  126.1 16.7 %copy-start.6 = (bf16[768,1024]{1,0:T(8,128)(2,1)}, bf16[768,1024]{1,0:T(8,128)(2,1)S(1)}, u32[]{:S(2)}) copy-start(bf16[768,1024]{1,0:T(8,128)(2,1)S(1)} %get-tuple-element.6) | copy-start | bytes 4718596
  126.1 16.7 %copy-start.7 = (bf16[768,1024]{1,0:T(8,128)(2,1)}, bf16[768,1024]{1,0:T(8,128)(2,1)S(1)}, u32[]{:S(2)}) copy-start(bf16[768,1024]{1,0:T(8,128)(2,1)S(1)} %get-tuple-element.7) | copy-start | bytes 4718596
  168.6 54.2 %all-to-all-start.1 = ((bf16[16,48,1024]{2,1,0:T(8,128)(2,1)}), bf16[16,48,1024]{2,1,0:T(8,128)(2,1)S(1)}, u32[]{:S(2)}, u32[]{:S(2)}) async-start(bf16[16,48,1024]{2,1,0:T(8,128)(2,1)} %bitcast.63), calls=%async_computation.1 | async-start | bytes 3145728 | tf_op jit(solution)/shard_map/all_to_all | solution.py:44
  173.6 42.4 %copy-start.11 = (bf16[768,2048]{1,0:T(8,128)(2,1)S(1)}, bf16[768,2048]{1,0:T(8,128)(2,1)}, u32[]{:S(2)}) copy-start(bf16[768,2048]{1,0:T(8,128)(2,1)} %fusion.10) | copy-start | bytes 9437188
  180.3 35.7 %collective-permute-start.3 = (bf16[768,1024]{1,0:T(8,128)(2,1)S(1)}, bf16[768,1024]{1,0:T(8,128)(2,1)S(1)}, u32[]{:S(2)}, u32[]{:S(2)}) collective-permute-start(bf16[768,1024]{1,0:T(8,128)(2,1)S(1)} %fusion.34), channel_id=1, source_target_pairs={{0,1},{1,0},{2,3},{3,2},{4,5},{5,4},{6,7},{7,6},{8,9},{9,8},{10,11... | collective-permute-start | bytes 4718600 | tf_op jit(solution)/shard_map/ppermute | solution.py:14
  222.8 43.1 %all-to-all-start.3 = ((bf16[16,48,1024]{2,1,0:T(8,128)(2,1)}), bf16[16,48,1024]{2,1,0:T(8,128)(2,1)}, u32[]{:S(2)}, u32[]{:S(2)}) async-start(bf16[16,48,1024]{2,1,0:T(8,128)(2,1)} %bitcast.62), calls=%async_computation.3 | async-start | bytes 3145728 | tf_op jit(solution)/shard_map/all_to_all | solution.py:44
  229.6 12.5 %copy-start.3 = (bf16[768,1024]{1,0:T(8,128)(2,1)S(1)}, bf16[768,1024]{1,0:T(8,128)(2,1)}, u32[]{:S(2)}) copy-start(bf16[768,1024]{1,0:T(8,128)(2,1)} %copy-done.2) | copy-start | bytes 4718596
  229.7 12.5 %copy-start.5 = (bf16[768,1024]{1,0:T(8,128)(2,1)S(1)}, bf16[768,1024]{1,0:T(8,128)(2,1)}, u32[]{:S(2)}) copy-start(bf16[768,1024]{1,0:T(8,128)(2,1)} %copy-done.4) | copy-start | bytes 4718596
  229.7 12.5 %copy-start.12 = (bf16[768,2048]{1,0:T(8,128)(2,1)S(1)}, bf16[768,2048]{1,0:T(8,128)(2,1)}, u32[]{:S(2)}) copy-start(bf16[768,2048]{1,0:T(8,128)(2,1)} %fusion.10) | copy-start | bytes 9437188
  251.7 19.1 %copy-start.1 = (bf16[256,2048]{1,0:T(8,128)(2,1)S(1)}, bf16[256,2048]{1,0:T(8,128)(2,1)}, u32[]{:S(2)}) copy-start(bf16[256,2048]{1,0:T(8,128)(2,1)} %param.6) | copy-start | bytes 3145732

commit v2 on v1

--- a/solution.py
+++ b/solution.py
@@ -38,6 +38,22 @@
     moving = swap(product(lax.dynamic_slice_in_dim(weight, (1 - me) * width, width, axis)))
     kept = product(lax.dynamic_slice_in_dim(weight, me * width, width, axis))
     return (kept.astype(jnp.float32) + moving.astype(jnp.float32)).astype(jnp.bfloat16)
+
+
+def sent_outputs(rows, weight):
+    if lax.axis_size("hidden") != 2:
+        return summed_features(rows, weight, 0)
+    return jnp.dot(rows, weight, preferred_element_type=jnp.float32).astype(jnp.bfloat16)
+
+
+def summed_mixed(mixed):
+    if lax.axis_size("hidden") != 2:
+        return mixed
+    width = mixed.shape[1] // 2
+    first = lax.axis_index("hidden") == 0
+    low, high = mixed[:, :width], mixed[:, width:]
+    moving = swap(jnp.where(first, high, low).astype(jnp.bfloat16))
+    return jnp.where(first, low, high) + moving.astype(jnp.float32)
 
 
 def exchange(block):
@@ -98,7 +114,7 @@
         pre_act = jnp.dot(expert_in, up_local, preferred_element_type=jnp.float32)
         activated, gelu_back = jax.vjp(gelu_fn, pre_act)
         hidden_act = activated.astype(jnp.bfloat16)
-        returned.append(exchange(summed_features(hidden_act, down_local, 0)))
+        returned.append(exchange(sent_outputs(hidden_act, down_local)))
         expert_ins.append(expert_in)
         hidden_acts.append(hidden_act)
         backs.append(gelu_back)
@@ -135,7 +151,7 @@
     mixed = sum(gates[:, k : k + 1] * picked(k, returned) for k in range(top_count))
     grad_tokens = sum(picked(k, input_back) for k in range(top_count))
     return (
-        mixed.astype(jnp.bfloat16),
+        summed_mixed(mixed).astype(jnp.bfloat16),
         grad_tokens.astype(jnp.bfloat16),
         grad_up[None],
         grad_down[None],

time: 271 us -> 242 us (0.89)
  waiting for transfers between devices: 153 us -> 124 us
  matrix products: 86.5 us -> 79.3 us
  other arithmetic: 3.69 us -> 6.88 us
  local copies, waits for them, and re-layouts: 1.62 us -> 4.68 us
    ppermute x4, waiting for transfers between devices: 70.6 us -> 44.8 us  [swap(): return lax.ppermute(block, 'hidden', [(0, 1), (1, 0)])]
    dot_general x4 -> x2, matrix products: 26.5 us -> 13.5 us  [product(): lax.dot_general(rows, part, (((1,), (contract,)), ((), ())), preferred_el...]
    dot_general x0 -> x1, matrix products: none -> 8.7 us  [sent_outputs(): jnp.dot(rows, weight, preferred_element_type=jnp.float32)]
    unnamed x31 -> x35, local copies, waits for them, and re-layouts: 0.88 us -> 3.96 us
    convert_element_type x0 -> x2, other arithmetic: none -> 2.98 us  [the longest x1 2.09 us: per_device(): summed_mixed(mixed).astype(jnp.bfloat16)]
  transfers between devices with their start and end apart: 8 -> 8, of which waited for: 6 -> 5; matrix products, arithmetic and copies ran while one was open for 27% -> 34% of each run, Pallas kernels for 0% -> 0%
where the time goes in v2:
time: 242 us; the launch traced here: 241 us
  waiting for transfers between devices  124 us (51%)
  matrix products  79.3 us (33%)
  starting transfers between devices  24.5 us (10%)
  other arithmetic  6.88 us (3%)
  local copies, waits for them, and re-layouts  4.68 us (2%)
    all_to_all x4, waiting for transfers between devices, exchange(): lax.all_to_all(block, 'expert', split_axis=0, concat_axis=0, tiled=True)  79.6 us
    ppermute x4, waiting for transfers between devices, swap(): return lax.ppermute(block, 'hidden', [(0, 1), (1, 0)])  44.8 us
    all_to_all x4, starting transfers between devices, exchange(): lax.all_to_all(block, 'expert', split_axis=0, concat_axis=0, tiled=True)  23.4 us
    dot_general x2, matrix products, outer(): lax.dot_general(jnp.concatenate(left, axis=0), jnp.concatenate(right, axi...  22 us
    dot_general x1, matrix products, per_device(): lax.dot_general(grad_out, down_local, (((1,), (1,)), ((), ())), preferred...  14.4 us
    dot_general x2, matrix products, product(): lax.dot_general(rows, part, (((1,), (contract,)), ((), ())), preferred_el...  13.5 us
    dot_general x1, matrix products, per_device(): pre_act = jnp.dot(expert_in, up_local, preferred_element_type=jnp.float32)  9.5 us
    dot_general x1, matrix products, sent_outputs(): jnp.dot(rows, weight, preferred_element_type=jnp.float32)  8.7 us
  transfers between devices with their start and end apart: 8, of which 5 were waited for; matrix products, arithmetic and copies ran while one was open for 34% of the time, Pallas kernels for 0%

profile of v2, /device:TPU:15, one launch (start us, length us, event | category | flops | bytes accessed | tf_op | source)
XLA Modules:
  0.0 240.8 jit_solution(9989910086392899211)
XLA Ops:
  0.7 0.9 copy.13
  2.0 0.7 broadcast_multiply_fusion
  3.7 1.7 convolution_convert_fusion.1
  5.4 6.6 %all-to-all-start = ((bf16[16,48,1024]{2,1,0:T(8,128)(2,1)}), bf16[16,48,1024]{2,1,0:T(8,128)(2,1)S(1)}, u32[]{:S(2)}, u32[]{:S(2)}) async-start(bf16[16,48,1024]{2,1,0:T(8,128)(2,1)} %bitcast.1), calls=%async_computation | async-start | bytes 3145728 | tf_op jit(solution)/shard_map/all_to_all | solution.py:60
  12.5 2.1 convolution_convert_fusion
  14.6 33.5 %all-to-all-done = bf16[16,48,1024]{2,1,0:T(8,128)(2,1)S(1)} async-done(((bf16[16,48,1024]{2,1,0:T(8,128)(2,1)}), bf16[16,48,1024]{2,1,0:T(8,128)(2,1)S(1)}, u32[]{:S(2)}, u32[]{:S(2)}) %all-to-all-start) | async-done | bytes 1572896 | tf_op jit(solution)/shard_map/all_to_all | solution.py:60
  48.1 4.9 %all-to-all-start.2 = ((bf16[16,48,1024]{2,1,0:T(8,128)(2,1)}), bf16[16,48,1024]{2,1,0:T(8,128)(2,1)}, u32[]{:S(2)}, u32[]{:S(2)}) async-start(bf16[16,48,1024]{2,1,0:T(8,128)(2,1)} %bitcast.8), calls=%async_computation.2 | async-start | bytes 3145728 | tf_op jit(solution)/shard_map/all_to_all | solution.py:60
  53.3 36.2 %all-to-all-done.2 = bf16[16,48,1024]{2,1,0:T(8,128)(2,1)} async-done(((bf16[16,48,1024]{2,1,0:T(8,128)(2,1)}), bf16[16,48,1024]{2,1,0:T(8,128)(2,1)}, u32[]{:S(2)}, u32[]{:S(2)}) %all-to-all-start.2) | async-done | bytes 1572896 | tf_op jit(solution)/shard_map/all_to_all | solution.py:60
  89.7 0.3 broadcast_select_fusion.3
  90.1 1.2 copy-done.4
  91.2 0.5 copy-done.6
  91.7 9.5 %fusion.4 = f32[768,2048]{1,0:T(8,128)S(1)} fusion(bf16[1,2048,2048]{2,1,0:T(8,128)(2,1)} %param.9, bf16[768,1024]{1,0:T(8,128)(2,1)S(1)} %get-tuple-element.9, bf16[768,1024]{1,0:T(8,128)(2,1)S(1)} %get-tuple-element.8), kind=kOutput, calls=%fused_computation.6 | convolution fusion | flops 6448742400 | bytes 17825792 | tf_op jit(solution)/shard_map/dot_general | solution.py:114
  101.3 8.7 %fusion.19 = bf16[768,2048]{1,0:T(8,128)(2,1)} fusion(bf16[1,2048,2048]{2,1,0:T(8,128)(2,1)S(1)} %bitcast.59, f32[768,2048]{1,0:T(8,128)S(1)} %fusion.4), kind=kOutput, calls=%fused_computation.24 | convolution fusion | flops 6458179584 | bytes 17825792 | tf_op jit(solution)/shard_map/dot_general | solution.py:46
  110.0 5.8 %all-to-all-start.1 = ((bf16[16,48,2048]{2,1,0:T(8,128)(2,1)}), bf16[16,48,2048]{2,1,0:T(8,128)(2,1)S(1)}, u32[]{:S(2)}, u32[]{:S(2)}) async-start(bf16[16,48,2048]{2,1,0:T(8,128)(2,1)} %bitcast.52), calls=%async_computation.1 | async-start | bytes 6291456 | tf_op jit(solution)/shard_map/all_to_all | solution.py:60
  115.7 10.0 %collective-permute-done.2 = bf16[768,1024]{1,0:T(8,128)(2,1)} collective-permute-done((bf16[768,1024]{1,0:T(8,128)(2,1)}, bf16[768,1024]{1,0:T(8,128)(2,1)}, u32[]{:S(2)}, u32[]{:S(2)}) %collective-permute-start.2) | collective-permute-done | bytes 1572896 | tf_op jit(solution)/shard_map/ppermute | solution.py:14
  125.7 2.1 broadcast_select_fusion.1
  127.8 14.4 %fusion.12 = bf16[768,2048]{1,0:T(8,128)(2,1)S(1)} fusion(f32[768,2048]{1,0:T(8,128)} %copy-done.14, bf16[1,2048,2048]{2,1,0:T(8,128)(2,1)} %param.10, bf16[768,1024]{1,0:T(8,128)(2,1)S(1)} %get-tuple-element.7, bf16[768,1024]{1,0:T(8,128)(2,1)S(1)} %get-tuple-element.6), kind=kOutput, calls=%fused_computation.16 | convolution fusion | flops 6480199680 | bytes 20971520 | tf_op jit(solution)/shard_map/dot_general | solution.py:123
  142.3 6.8 %fusion.28 = bf16[768,1024]{1,0:T(8,128)(2,1)S(1)} fusion(bf16[768,2048]{1,0:T(8,128)(2,1)S(1)} %fusion.12, bf16[1,2048,2048]{2,1,0:T(8,128)(2,1)} %param.9, s32[]{:T(128)S(6)} %select_n.89), kind=kOutput, calls=%fused_computation.33 | convolution fusion | flops 3222011904 | bytes 8912900 | tf_op jit(solution)/shard_map/dot_general | solution.py:29
  149.1 0.3 collective-permute-start.3
  149.4 34.8 %collective-permute-done.3 = bf16[768,1024]{1,0:T(8,128)(2,1)S(1)} collective-permute-done((bf16[768,1024]{1,0:T(8,128)(2,1)S(1)}, bf16[768,1024]{1,0:T(8,128)(2,1)S(1)}, u32[]{:S(2)}, u32[]{:S(2)}) %collective-permute-start.3) | collective-permute-done | bytes 1572896 | tf_op jit(solution)/shard_map/ppermute | solution.py:14
  184.2 6.8 %add_convert_fusion = bf16[768,1024]{1,0:T(8,128)(2,1)} fusion(bf16[768,1024]{1,0:T(8,128)(2,1)S(1)} %collective-permute-done.3, bf16[768,2048]{1,0:T(8,128)(2,1)S(1)} %fusion.12, bf16[1,2048,2048]{2,1,0:T(8,128)(2,1)} %param.9, s32[]{:T(128)S(6)} %select_n.82), kind=kOutput, calls=%fused_computation.27 | convolution fusion | flops 3225157632 | bytes 10485764 | tf_op jit(solution)/shard_map/dot_general | solution.py:29
  191.0 6.1 %all-to-all-start.3 = ((bf16[16,48,1024]{2,1,0:T(8,128)(2,1)}), bf16[16,48,1024]{2,1,0:T(8,128)(2,1)}, u32[]{:S(2)}, u32[]{:S(2)}) async-start(bf16[16,48,1024]{2,1,0:T(8,128)(2,1)} %bitcast.53), calls=%async_computation.3 | async-start | bytes 3145728 | tf_op jit(solution)/shard_map/all_to_all | solution.py:60
  197.1 12.5 %convert_bitcast_fusion = bf16[1,2048,2048]{2,1,0:T(8,128)(2,1)} fusion(bf16[768,1024]{1,0:T(8,128)(2,1)} %copy-done.9, bf16[768,1024]{1,0:T(8,128)(2,1)} %copy-done.8, f32[768,2048]{1,0:T(8,128)} %copy-done.14), kind=kOutput, calls=%fused_computation.8 | convolution fusion | flops 6467092480 | bytes 17825792 | tf_op jit(solution)/shard_map/dot_general | solution.py:132
  209.6 9.5 %convert_bitcast_fusion.1 = bf16[1,2048,2048]{2,1,0:T(8,128)(2,1)} fusion(bf16[768,2048]{1,0:T(8,128)(2,1)S(1)} %copy-done.13, bf16[768,1024]{1,0:T(8,128)(2,1)S(1)} %copy-done.7, bf16[768,1024]{1,0:T(8,128)(2,1)S(1)} %copy-done.5), kind=kOutput, calls=%fused_computation.9 | convolution fusion | flops 6452936704 | bytes 14680064 | tf_op jit(solution)/shard_map/dot_general | solution.py:132
  219.2 1.0 convolution_multiply_fusion.1
  220.2 1.0 fusion.24
  221.3 1.3 copy-done.2
  222.6 0.9 select_convert_fusion
  223.8 9.9 %all-to-all-done.3 = bf16[16,48,1024]{2,1,0:T(8,128)(2,1)} async-done(((bf16[16,48,1024]{2,1,0:T(8,128)(2,1)}), bf16[16,48,1024]{2,1,0:T(8,128)(2,1)}, u32[]{:S(2)}, u32[]{:S(2)}) %all-to-all-start.3) | async-done | bytes 1572896 | tf_op jit(solution)/shard_map/all_to_all | solution.py:60
  233.7 2.1 fusion.43
  235.8 2.8 %fusion.31 = bf16[256,1024]{1,0:T(8,128)(2,1)} fusion(f32[256,1024]{1,0:T(8,128)S(1)} %fusion.43, bf16[768,1024]{1,0:T(8,128)(2,1)} %bitcast.13, s32[256]{0:T(256)S(1)} %get-tuple-element.5), kind=kOutput, calls=%fused_computation.42 | convolution fusion | flops 403374080 | bytes 3146752 | tf_op jit(solution)/shard_map/dot_general | solution.py:145
  238.7 2.1 add_convert_fusion.1
  (51 shorter events, 2.7 us)
Async XLA Ops:
  0.6 3.0 %copy-start = (bf16[256,2048]{1,0:T(8,128)(2,1)S(1)}, bf16[256,2048]{1,0:T(8,128)(2,1)}, u32[]{:S(2)}) copy-start(bf16[256,2048]{1,0:T(8,128)(2,1)} %param.6) | copy-start | bytes 3145732
  3.3 8.6 %copy-start.11 = (f32[256,2]{0,1:T(2,128)S(1)}, f32[256,2]{0,1:T(2,128)}, u32[]{:S(2)}) copy-start(f32[256,2]{0,1:T(2,128)} %param.7) | copy-start | bytes 6148
  3.6 8.6 %copy-start.10 = (bf16[256,1024]{1,0:T(8,128)(2,1)S(1)}, bf16[256,1024]{1,0:T(8,128)(2,1)}, u32[]{:S(2)}) copy-start(bf16[256,1024]{1,0:T(8,128)(2,1)} %param.11) | copy-start | bytes 1572868
  5.4 42.7 %all-to-all-start = ((bf16[16,48,1024]{2,1,0:T(8,128)(2,1)}), bf16[16,48,1024]{2,1,0:T(8,128)(2,1)S(1)}, u32[]{:S(2)}, u32[]{:S(2)}) async-start(bf16[16,48,1024]{2,1,0:T(8,128)(2,1)} %bitcast.1), calls=%async_computation | async-start | bytes 3145728 | tf_op jit(solution)/shard_map/all_to_all | solution.py:60
  48.1 41.3 %all-to-all-start.2 = ((bf16[16,48,1024]{2,1,0:T(8,128)(2,1)}), bf16[16,48,1024]{2,1,0:T(8,128)(2,1)}, u32[]{:S(2)}, u32[]{:S(2)}) async-start(bf16[16,48,1024]{2,1,0:T(8,128)(2,1)} %bitcast.8), calls=%async_computation.2 | async-start | bytes 3145728 | tf_op jit(solution)/shard_map/all_to_all | solution.py:60
  53.0 36.7 %collective-permute-start = (bf16[768,1024]{1,0:T(8,128)(2,1)S(1)}, bf16[768,1024]{1,0:T(8,128)(2,1)S(1)}, u32[]{:S(2)}, u32[]{:S(2)}) collective-permute-start(bf16[768,1024]{1,0:T(8,128)(2,1)S(1)} %bitcast.51), channel_id=1, source_target_pairs={{0,1},{1,0},{2,3},{3,2},{4,5},{5,4},{6,7},{7,6},{8,9},{9,8},{10,11... | collective-permute-start | bytes 4718600 | tf_op jit(solution)/shard_map/ppermute | solution.py:14
  89.5 36.3 %collective-permute-start.2 = (bf16[768,1024]{1,0:T(8,128)(2,1)}, bf16[768,1024]{1,0:T(8,128)(2,1)}, u32[]{:S(2)}, u32[]{:S(2)}) collective-permute-start(bf16[768,1024]{1,0:T(8,128)(2,1)} %bitcast.9), channel_id=1, source_target_pairs={{0,1},{1,0},{2,3},{3,2},{4,5},{5,4},{6,7},{7,6},{8,9},{9,8},{10,11... | collective-permute-start | bytes 4718600 | tf_op jit(solution)/shard_map/ppermute | solution.py:14
  89.7 11.5 %slice-start = ((s8[8388608]{0:T(1024)(128)(4,1)}), s8[4194304]{0:T(1024)(128)(4,1)S(1)}, s32[]{:S(2)}) async-start(s8[8388608]{0:T(1024)(128)(4,1)} %bitcast.58), calls=%async_computation.4 | async-start | bytes 8388608
  90.0 1.2 copy-start.4
  90.1 1.7 copy-start.6
  91.7 9.5 %slice-start.1 = ((s8[8388608]{0:T(1024)(128)(4,1)}), s8[4194304]{0:T(1024)(128)(4,1)S(1)}, s32[]{:S(2)}) async-start(s8[8388608]{0:T(1024)(128)(4,1)} %bitcast.58), calls=%async_computation.5 | async-start | bytes 8388608
  101.2 8.7 %copy-start.14 = (f32[768,2048]{1,0:T(8,128)}, f32[768,2048]{1,0:T(8,128)S(1)}, u32[]{:S(2)}) copy-start(f32[768,2048]{1,0:T(8,128)S(1)} %fusion.4) | copy-start | bytes 18874372
  110.0 81.0 %all-to-all-start.1 = ((bf16[16,48,2048]{2,1,0:T(8,128)(2,1)}), bf16[16,48,2048]{2,1,0:T(8,128)(2,1)S(1)}, u32[]{:S(2)}, u32[]{:S(2)}) async-start(bf16[16,48,2048]{2,1,0:T(8,128)(2,1)} %bitcast.52), calls=%async_computation.1 | async-start | bytes 6291456 | tf_op jit(solution)/shard_map/all_to_all | solution.py:60
  127.8 14.5 %copy-start.8 = (bf16[768,1024]{1,0:T(8,128)(2,1)}, bf16[768,1024]{1,0:T(8,128)(2,1)S(1)}, u32[]{:S(2)}) copy-start(bf16[768,1024]{1,0:T(8,128)(2,1)S(1)} %get-tuple-element.6) | copy-start | bytes 4718596
  127.8 14.5 %copy-start.9 = (bf16[768,1024]{1,0:T(8,128)(2,1)}, bf16[768,1024]{1,0:T(8,128)(2,1)S(1)}, u32[]{:S(2)}) copy-start(bf16[768,1024]{1,0:T(8,128)(2,1)S(1)} %get-tuple-element.7) | copy-start | bytes 4718596
  142.3 41.9 %copy-start.12 = (bf16[768,2048]{1,0:T(8,128)(2,1)}, bf16[768,2048]{1,0:T(8,128)(2,1)S(1)}, u32[]{:S(2)}) copy-start(bf16[768,2048]{1,0:T(8,128)(2,1)S(1)} %fusion.12) | copy-start | bytes 9437188
  149.1 35.1 %collective-permute-start.3 = (bf16[768,1024]{1,0:T(8,128)(2,1)S(1)}, bf16[768,1024]{1,0:T(8,128)(2,1)S(1)}, u32[]{:S(2)}, u32[]{:S(2)}) collective-permute-start(bf16[768,1024]{1,0:T(8,128)(2,1)S(1)} %fusion.28), channel_id=1, source_target_pairs={{0,1},{1,0},{2,3},{3,2},{4,5},{5,4},{6,7},{7,6},{8,9},{9,8},{10,11... | collective-permute-start | bytes 4718600 | tf_op jit(solution)/shard_map/ppermute | solution.py:14
  191.0 42.7 %all-to-all-start.3 = ((bf16[16,48,1024]{2,1,0:T(8,128)(2,1)}), bf16[16,48,1024]{2,1,0:T(8,128)(2,1)}, u32[]{:S(2)}, u32[]{:S(2)}) async-start(bf16[16,48,1024]{2,1,0:T(8,128)(2,1)} %bitcast.53), calls=%async_computation.3 | async-start | bytes 3145728 | tf_op jit(solution)/shard_map/all_to_all | solution.py:60
  197.1 12.5 %copy-start.5 = (bf16[768,1024]{1,0:T(8,128)(2,1)S(1)}, bf16[768,1024]{1,0:T(8,128)(2,1)}, u32[]{:S(2)}) copy-start(bf16[768,1024]{1,0:T(8,128)(2,1)} %copy-done.4) | copy-start | bytes 4718596
  197.1 12.5 %copy-start.7 = (bf16[768,1024]{1,0:T(8,128)(2,1)S(1)}, bf16[768,1024]{1,0:T(8,128)(2,1)}, u32[]{:S(2)}) copy-start(bf16[768,1024]{1,0:T(8,128)(2,1)} %copy-done.6) | copy-start | bytes 4718596
  197.1 12.5 %copy-start.13 = (bf16[768,2048]{1,0:T(8,128)(2,1)S(1)}, bf16[768,2048]{1,0:T(8,128)(2,1)}, u32[]{:S(2)}) copy-start(bf16[768,2048]{1,0:T(8,128)(2,1)} %copy-done.12) | copy-start | bytes 9437188
  221.3 1.4 copy-start.2
  223.5 15.2 %copy-start.3 = (f32[256,2048]{1,0:T(8,128)S(1)}, f32[256,2048]{1,0:T(8,128)}, u32[]{:S(2)}) copy-start(f32[256,2048]{1,0:T(8,128)} %copy-done.2) | copy-start | bytes 6291460
  223.5 15.2 %collective-permute-start.1 = (bf16[256,1024]{1,0:T(8,128)(2,1)}, bf16[256,1024]{1,0:T(8,128)(2,1)}, u32[]{:S(2)}, u32[]{:S(2)}) collective-permute-start(bf16[256,1024]{1,0:T(8,128)(2,1)} %select_convert_fusion), channel_id=1, source_target_pairs={{0,1},{1,0},{2,3},{3,2},{4,5},{5,4},{6,7},{7,6},{8,9},{9,8},{10,11... | collective-permute-start | bytes 1572872 | tf_op jit(solution)/shard_map/ppermute | solution.py:14
  233.7 7.1 %copy-start.1 = (bf16[256,2048]{1,0:T(8,128)(2,1)S(1)}, bf16[256,2048]{1,0:T(8,128)(2,1)}, u32[]{:S(2)}) copy-start(bf16[256,2048]{1,0:T(8,128)(2,1)} %param.6) | copy-start | bytes 3145732

commit v3 on v2

--- a/solution.py
+++ b/solution.py
@@ -36,7 +36,9 @@
     width = weight.shape[axis] // 2
     me = lax.axis_index("hidden")
     moving = swap(product(lax.dynamic_slice_in_dim(weight, (1 - me) * width, width, axis)))
-    kept = product(lax.dynamic_slice_in_dim(weight, me * width, width, axis))
+    kept = lax.optimization_barrier(
+        product(lax.dynamic_slice_in_dim(weight, me * width, width, axis))
+    )
     return (kept.astype(jnp.float32) + moving.astype(jnp.float32)).astype(jnp.bfloat16)
 
 
@@ -139,17 +141,17 @@
     grad_down = outer(hidden_acts, grad_outs)
     grad_up = outer(expert_ins, grad_pres)
 
-    def picked(which, arrays):
+    def picked(chosen, arrays):
         total = None
-        for pick, array in zip(picks, arrays):
+        for pick, array in zip(chosen, arrays):
             part = lax.dot_general(
-                pick[which], array, (((0,), (0,)), ((), ())), preferred_element_type=jnp.float32
+                pick, array, (((0,), (0,)), ((), ())), preferred_element_type=jnp.float32
             )
             total = part if total is None else total + part
         return total
 
-    mixed = sum(gates[:, k : k + 1] * picked(k, returned) for k in range(top_count))
-    grad_tokens = sum(picked(k, input_back) for k in range(top_count))
+    mixed = sum(gates[:, k : k + 1] * picked([pick[k] for pick in picks], returned) for k in range(top_count))
+    grad_tokens = picked([sum(pick[1:], pick[0]) for pick in picks], input_back)
     return (
         summed_mixed(mixed).astype(jnp.bfloat16),
         grad_tokens.astype(jnp.bfloat16),

time: 242 us -> 234 us (0.967)
  waiting for transfers between devices: 124 us -> 114 us
  other arithmetic: 6.88 us -> 10.5 us
    ppermute x4, waiting for transfers between devices: 44.8 us -> 38.3 us  [swap(): return lax.ppermute(block, 'hidden', [(0, 1), (1, 0)])]
    dot_general x2, matrix products: 22 us -> 26.4 us  [outer(): lax.dot_general(jnp.concatenate(left, axis=0), jnp.concatenate(right, axi...]
    all_to_all x4, waiting for transfers between devices: 79.6 us -> 75.4 us  [exchange(): lax.all_to_all(block, 'expert', split_axis=0, concat_axis=0, tiled=True)]
    dot_general x4 -> x3, matrix products: 7.02 us -> 4.91 us  [picked(): lax.dot_general(pick, array, (((0,), (0,)), ((), ())), preferred_element_...]
  transfers between devices with their start and end apart: 8 -> 8, of which waited for: 5 -> 6; matrix products, arithmetic and copies ran while one was open for 34% -> 37% of each run, Pallas kernels for 0% -> 0%
where the time goes in v3:
time: 234 us; the launch traced here: 233 us
  waiting for transfers between devices  114 us (49%)
  matrix products  81.3 us (35%)
  starting transfers between devices  24 us (10%)
  other arithmetic  10.5 us (4%)
  local copies, waits for them, and re-layouts  3.07 us (1%)
    all_to_all x4, waiting for transfers between devices, exchange(): lax.all_to_all(block, 'expert', split_axis=0, concat_axis=0, tiled=True)  75.4 us
    ppermute x4, waiting for transfers between devices, swap(): return lax.ppermute(block, 'hidden', [(0, 1), (1, 0)])  38.3 us
    dot_general x2, matrix products, outer(): lax.dot_general(jnp.concatenate(left, axis=0), jnp.concatenate(right, axi...  26.4 us
    all_to_all x4, starting transfers between devices, exchange(): lax.all_to_all(block, 'expert', split_axis=0, concat_axis=0, tiled=True)  22.9 us
    dot_general x1, matrix products, per_device(): lax.dot_general(grad_out, down_local, (((1,), (1,)), ((), ())), preferred...  14.4 us
    dot_general x2, matrix products, product(): lax.dot_general(rows, part, (((1,), (contract,)), ((), ())), preferred_el...  12.4 us
    dot_general x1, matrix products, per_device(): pre_act = jnp.dot(expert_in, up_local, preferred_element_type=jnp.float32)  10.3 us
    dot_general x1, matrix products, sent_outputs(): jnp.dot(rows, weight, preferred_element_type=jnp.float32)  8.7 us
  transfers between devices with their start and end apart: 8, of which 6 were waited for; matrix products, arithmetic and copies ran while one was open for 37% of the time, Pallas kernels for 0%

profile of v3, /device:TPU:15, one launch (start us, length us, event | category | flops | bytes accessed | tf_op | source)
XLA Modules:
  0.0 233.5 jit_solution(1279329996668938179)
XLA Ops:
  0.7 0.9 copy.13
  1.7 0.3 fusion.31
  2.0 0.7 broadcast_multiply_fusion
  3.7 1.7 convolution_convert_fusion.1
  5.4 6.6 %all-to-all-start = ((bf16[16,48,1024]{2,1,0:T(8,128)(2,1)}), bf16[16,48,1024]{2,1,0:T(8,128)(2,1)S(1)}, u32[]{:S(2)}, u32[]{:S(2)}) async-start(bf16[16,48,1024]{2,1,0:T(8,128)(2,1)} %bitcast.1), calls=%async_computation | async-start | bytes 3145728 | tf_op jit(solution)/shard_map/all_to_all | solution.py:62
  12.5 2.1 convolution_convert_fusion
  14.6 33.5 %all-to-all-done = bf16[16,48,1024]{2,1,0:T(8,128)(2,1)S(1)} async-done(((bf16[16,48,1024]{2,1,0:T(8,128)(2,1)}), bf16[16,48,1024]{2,1,0:T(8,128)(2,1)S(1)}, u32[]{:S(2)}, u32[]{:S(2)}) %all-to-all-start) | async-done | bytes 1572896 | tf_op jit(solution)/shard_map/all_to_all | solution.py:62
  48.1 4.9 %all-to-all-start.2 = ((bf16[16,48,1024]{2,1,0:T(8,128)(2,1)}), bf16[16,48,1024]{2,1,0:T(8,128)(2,1)}, u32[]{:S(2)}, u32[]{:S(2)}) async-start(bf16[16,48,1024]{2,1,0:T(8,128)(2,1)} %bitcast.8), calls=%async_computation.2 | async-start | bytes 3145728 | tf_op jit(solution)/shard_map/all_to_all | solution.py:62
  53.3 36.2 %all-to-all-done.2 = bf16[16,48,1024]{2,1,0:T(8,128)(2,1)} async-done(((bf16[16,48,1024]{2,1,0:T(8,128)(2,1)}), bf16[16,48,1024]{2,1,0:T(8,128)(2,1)}, u32[]{:S(2)}, u32[]{:S(2)}) %all-to-all-start.2) | async-done | bytes 1572896 | tf_op jit(solution)/shard_map/all_to_all | solution.py:62
  89.7 2.0 broadcast_select_fusion.3
  91.8 10.3 %fusion.4 = f32[768,2048]{1,0:T(8,128)S(1)} fusion(bf16[1,2048,2048]{2,1,0:T(8,128)(2,1)} %param.9, bf16[768,1024]{1,0:T(8,128)(2,1)} %get-tuple-element.9, bf16[768,1024]{1,0:T(8,128)(2,1)} %get-tuple-element.8), kind=kOutput, calls=%fused_computation.6 | convolution fusion | flops 6448742400 | bytes 17825792 | tf_op jit(solution)/shard_map/dot_general | solution.py:116
  102.2 8.7 %fusion.19 = bf16[768,2048]{1,0:T(8,128)(2,1)} fusion(bf16[1,2048,2048]{2,1,0:T(8,128)(2,1)S(1)} %bitcast.56, f32[768,2048]{1,0:T(8,128)S(1)} %fusion.4), kind=kOutput, calls=%fused_computation.24 | convolution fusion | flops 6458179584 | bytes 17825792 | tf_op jit(solution)/shard_map/dot_general | solution.py:48
  110.9 5.8 %all-to-all-start.1 = ((bf16[16,48,2048]{2,1,0:T(8,128)(2,1)}), bf16[16,48,2048]{2,1,0:T(8,128)(2,1)S(1)}, u32[]{:S(2)}, u32[]{:S(2)}) async-start(bf16[16,48,2048]{2,1,0:T(8,128)(2,1)} %bitcast.50), calls=%async_computation.1 | async-start | bytes 6291456 | tf_op jit(solution)/shard_map/all_to_all | solution.py:62
  116.7 9.1 %collective-permute-done.2 = bf16[768,1024]{1,0:T(8,128)(2,1)} collective-permute-done((bf16[768,1024]{1,0:T(8,128)(2,1)}, bf16[768,1024]{1,0:T(8,128)(2,1)}, u32[]{:S(2)}, u32[]{:S(2)}) %collective-permute-start.2) | collective-permute-done | bytes 1572896 | tf_op jit(solution)/shard_map/ppermute | solution.py:14
  125.7 2.1 broadcast_select_fusion.1
  127.8 14.4 %fusion.12 = bf16[768,2048]{1,0:T(8,128)(2,1)S(1)} fusion(f32[768,2048]{1,0:T(8,128)} %copy-done.11, bf16[1,2048,2048]{2,1,0:T(8,128)(2,1)} %param.10, bf16[768,1024]{1,0:T(8,128)(2,1)S(1)} %get-tuple-element.7, bf16[768,1024]{1,0:T(8,128)(2,1)S(1)} %get-tuple-element.6), kind=kOutput, calls=%fused_computation.16 | convolution fusion | flops 6480199680 | bytes 20971520 | tf_op jit(solution)/shard_map/dot_general | solution.py:125
  142.3 6.8 %fusion.28 = bf16[768,1024]{1,0:T(8,128)(2,1)S(1)} fusion(bf16[768,2048]{1,0:T(8,128)(2,1)S(1)} %fusion.12, bf16[1,2048,2048]{2,1,0:T(8,128)(2,1)} %param.9, s32[]{:T(128)S(6)} %select_n.89), kind=kOutput, calls=%fused_computation.33 | convolution fusion | flops 3222011904 | bytes 8912900 | tf_op jit(solution)/shard_map/dot_general | solution.py:29
  149.1 0.3 collective-permute-start.3
  149.4 5.6 %fusion.25 = bf16[768,1024]{1,0:T(8,128)(2,1)S(1)} fusion(bf16[768,2048]{1,0:T(8,128)(2,1)S(1)} %fusion.12, bf16[1,2048,2048]{2,1,0:T(8,128)(2,1)} %param.9, s32[]{:T(128)S(6)} %select_n.82), kind=kOutput, calls=%fused_computation.32 | convolution fusion | flops 3222011904 | bytes 8912900 | tf_op jit(solution)/shard_map/dot_general | solution.py:29
  155.1 29.2 %collective-permute-done.3 = bf16[768,1024]{1,0:T(8,128)(2,1)S(1)} collective-permute-done((bf16[768,1024]{1,0:T(8,128)(2,1)S(1)}, bf16[768,1024]{1,0:T(8,128)(2,1)S(1)}, u32[]{:S(2)}, u32[]{:S(2)}) %collective-permute-start.3) | collective-permute-done | bytes 1572896 | tf_op jit(solution)/shard_map/ppermute | solution.py:14
  184.2 1.9 add_convert_fusion
  186.1 0.4 all-to-all-done.1
  186.5 5.7 %all-to-all-start.3 = ((bf16[16,48,1024]{2,1,0:T(8,128)(2,1)}), bf16[16,48,1024]{2,1,0:T(8,128)(2,1)}, u32[]{:S(2)}, u32[]{:S(2)}) async-start(bf16[16,48,1024]{2,1,0:T(8,128)(2,1)} %bitcast.49), calls=%async_computation.3 | async-start | bytes 3145728 | tf_op jit(solution)/shard_map/all_to_all | solution.py:62
  192.2 11.4 %convert_bitcast_fusion.1 = bf16[1,2048,2048]{2,1,0:T(8,128)(2,1)} fusion(bf16[768,2048]{1,0:T(8,128)(2,1)} %copy-done.10, bf16[768,1024]{1,0:T(8,128)(2,1)} %get-tuple-element.9, bf16[768,1024]{1,0:T(8,128)(2,1)} %get-tuple-element.8), kind=kOutput, calls=%fused_computation.9 | convolution fusion | flops 6452936704 | bytes 14680064 | tf_op jit(solution)/shard_map/dot_general | solution.py:134
  203.6 1.0 convolution_multiply_fusion.1
  204.7 1.0 fusion.24
  205.7 1.4 copy-done.2
  207.1 0.9 select_convert_fusion
  208.3 15.0 %convert_bitcast_fusion = bf16[1,2048,2048]{2,1,0:T(8,128)(2,1)} fusion(bf16[768,1024]{1,0:T(8,128)(2,1)S(1)} %copy-done.7, bf16[768,1024]{1,0:T(8,128)(2,1)S(1)} %copy-done.5, f32[768,2048]{1,0:T(8,128)} %copy-done.11), kind=kOutput, calls=%fused_computation.8 | convolution fusion | flops 6467092480 | bytes 17825792 | tf_op jit(solution)/shard_map/dot_general | solution.py:134
  223.3 5.3 %all-to-all-done.3 = bf16[16,48,1024]{2,1,0:T(8,128)(2,1)} async-done(((bf16[16,48,1024]{2,1,0:T(8,128)(2,1)}), bf16[16,48,1024]{2,1,0:T(8,128)(2,1)}, u32[]{:S(2)}, u32[]{:S(2)}) %all-to-all-start.3) | async-done | bytes 1572896 | tf_op jit(solution)/shard_map/all_to_all | solution.py:62
  228.5 2.8 %convolution_convert_fusion.2 = bf16[256,1024]{1,0:T(8,128)(2,1)} fusion(bf16[768,1024]{1,0:T(8,128)(2,1)} %bitcast.13, s32[256]{0:T(256)S(1)} %get-tuple-element.5, s32[256]{0:T(256)S(1)} %get-tuple-element.4), kind=kOutput, calls=%fused_computation.41 | convolution fusion | flops 404488192 | bytes 2099200 | tf_op jit(solution)/shard_map/dot_general | solution.py:147
  231.4 2.1 add_convert_fusion.1
  (45 shorter events, 2.4 us)
Async XLA Ops:
  0.6 3.0 %copy-start = (bf16[256,2048]{1,0:T(8,128)(2,1)S(1)}, bf16[256,2048]{1,0:T(8,128)(2,1)}, u32[]{:S(2)}) copy-start(bf16[256,2048]{1,0:T(8,128)(2,1)} %param.6) | copy-start | bytes 3145732
  3.3 8.6 %copy-start.9 = (f32[256,2]{0,1:T(2,128)S(1)}, f32[256,2]{0,1:T(2,128)}, u32[]{:S(2)}) copy-start(f32[256,2]{0,1:T(2,128)} %param.7) | copy-start | bytes 6148
  3.6 8.6 %copy-start.8 = (bf16[256,1024]{1,0:T(8,128)(2,1)S(1)}, bf16[256,1024]{1,0:T(8,128)(2,1)}, u32[]{:S(2)}) copy-start(bf16[256,1024]{1,0:T(8,128)(2,1)} %param.11) | copy-start | bytes 1572868
  5.4 42.7 %all-to-all-start = ((bf16[16,48,1024]{2,1,0:T(8,128)(2,1)}), bf16[16,48,1024]{2,1,0:T(8,128)(2,1)S(1)}, u32[]{:S(2)}, u32[]{:S(2)}) async-start(bf16[16,48,1024]{2,1,0:T(8,128)(2,1)} %bitcast.1), calls=%async_computation | async-start | bytes 3145728 | tf_op jit(solution)/shard_map/all_to_all | solution.py:62
  48.1 41.3 %all-to-all-start.2 = ((bf16[16,48,1024]{2,1,0:T(8,128)(2,1)}), bf16[16,48,1024]{2,1,0:T(8,128)(2,1)}, u32[]{:S(2)}, u32[]{:S(2)}) async-start(bf16[16,48,1024]{2,1,0:T(8,128)(2,1)} %bitcast.8), calls=%async_computation.2 | async-start | bytes 3145728 | tf_op jit(solution)/shard_map/all_to_all | solution.py:62
  53.0 36.7 %collective-permute-start = (bf16[768,1024]{1,0:T(8,128)(2,1)S(1)}, bf16[768,1024]{1,0:T(8,128)(2,1)S(1)}, u32[]{:S(2)}, u32[]{:S(2)}) collective-permute-start(bf16[768,1024]{1,0:T(8,128)(2,1)S(1)} %bitcast.48), channel_id=1, source_target_pairs={{0,1},{1,0},{2,3},{3,2},{4,5},{5,4},{6,7},{7,6},{8,9},{9,8},{10,11... | collective-permute-start | bytes 4718600 | tf_op jit(solution)/shard_map/ppermute | solution.py:14
  89.5 36.3 %collective-permute-start.2 = (bf16[768,1024]{1,0:T(8,128)(2,1)}, bf16[768,1024]{1,0:T(8,128)(2,1)}, u32[]{:S(2)}, u32[]{:S(2)}) collective-permute-start(bf16[768,1024]{1,0:T(8,128)(2,1)} %bitcast.9), channel_id=1, source_target_pairs={{0,1},{1,0},{2,3},{3,2},{4,5},{5,4},{6,7},{7,6},{8,9},{9,8},{10,11... | collective-permute-start | bytes 4718600 | tf_op jit(solution)/shard_map/ppermute | solution.py:14
  89.7 12.4 %slice-start = ((s8[8388608]{0:T(1024)(128)(4,1)}), s8[4194304]{0:T(1024)(128)(4,1)S(1)}, s32[]{:S(2)}) async-start(s8[8388608]{0:T(1024)(128)(4,1)} %bitcast.55), calls=%async_computation.4 | async-start | bytes 8388608
  91.8 10.4 %slice-start.1 = ((s8[8388608]{0:T(1024)(128)(4,1)}), s8[4194304]{0:T(1024)(128)(4,1)S(1)}, s32[]{:S(2)}) async-start(s8[8388608]{0:T(1024)(128)(4,1)} %bitcast.55), calls=%async_computation.5 | async-start | bytes 8388608
  102.2 8.7 %copy-start.11 = (f32[768,2048]{1,0:T(8,128)}, f32[768,2048]{1,0:T(8,128)S(1)}, u32[]{:S(2)}) copy-start(f32[768,2048]{1,0:T(8,128)S(1)} %fusion.4) | copy-start | bytes 18874372
  110.9 75.7 %all-to-all-start.1 = ((bf16[16,48,2048]{2,1,0:T(8,128)(2,1)}), bf16[16,48,2048]{2,1,0:T(8,128)(2,1)S(1)}, u32[]{:S(2)}, u32[]{:S(2)}) async-start(bf16[16,48,2048]{2,1,0:T(8,128)(2,1)} %bitcast.50), calls=%async_computation.1 | async-start | bytes 6291456 | tf_op jit(solution)/shard_map/all_to_all | solution.py:62
  127.8 14.5 %copy-start.4 = (bf16[768,1024]{1,0:T(8,128)(2,1)}, bf16[768,1024]{1,0:T(8,128)(2,1)S(1)}, u32[]{:S(2)}) copy-start(bf16[768,1024]{1,0:T(8,128)(2,1)S(1)} %get-tuple-element.6) | copy-start | bytes 4718596
  127.8 14.5 %copy-start.6 = (bf16[768,1024]{1,0:T(8,128)(2,1)}, bf16[768,1024]{1,0:T(8,128)(2,1)S(1)}, u32[]{:S(2)}) copy-start(bf16[768,1024]{1,0:T(8,128)(2,1)S(1)} %get-tuple-element.7) | copy-start | bytes 4718596
  142.3 7.1 %copy-start.10 = (bf16[768,2048]{1,0:T(8,128)(2,1)}, bf16[768,2048]{1,0:T(8,128)(2,1)S(1)}, u32[]{:S(2)}) copy-start(bf16[768,2048]{1,0:T(8,128)(2,1)S(1)} %fusion.12) | copy-start | bytes 9437188
  149.1 35.1 %collective-permute-start.3 = (bf16[768,1024]{1,0:T(8,128)(2,1)S(1)}, bf16[768,1024]{1,0:T(8,128)(2,1)S(1)}, u32[]{:S(2)}, u32[]{:S(2)}) collective-permute-start(bf16[768,1024]{1,0:T(8,128)(2,1)S(1)} %fusion.28), channel_id=1, source_target_pairs={{0,1},{1,0},{2,3},{3,2},{4,5},{5,4},{6,7},{7,6},{8,9},{9,8},{10,11... | collective-permute-start | bytes 4718600 | tf_op jit(solution)/shard_map/ppermute | solution.py:14
  186.5 42.0 %all-to-all-start.3 = ((bf16[16,48,1024]{2,1,0:T(8,128)(2,1)}), bf16[16,48,1024]{2,1,0:T(8,128)(2,1)}, u32[]{:S(2)}, u32[]{:S(2)}) async-start(bf16[16,48,1024]{2,1,0:T(8,128)(2,1)} %bitcast.49), calls=%async_computation.3 | async-start | bytes 3145728 | tf_op jit(solution)/shard_map/all_to_all | solution.py:62
  204.6 3.6 %copy-start.5 = (bf16[768,1024]{1,0:T(8,128)(2,1)S(1)}, bf16[768,1024]{1,0:T(8,128)(2,1)}, u32[]{:S(2)}) copy-start(bf16[768,1024]{1,0:T(8,128)(2,1)} %copy-done.4) | copy-start | bytes 4718596
  204.7 3.6 %copy-start.7 = (bf16[768,1024]{1,0:T(8,128)(2,1)S(1)}, bf16[768,1024]{1,0:T(8,128)(2,1)}, u32[]{:S(2)}) copy-start(bf16[768,1024]{1,0:T(8,128)(2,1)} %copy-done.6) | copy-start | bytes 4718596
  205.7 1.4 copy-start.2
  208.0 23.4 %collective-permute-start.1 = (bf16[256,1024]{1,0:T(8,128)(2,1)}, bf16[256,1024]{1,0:T(8,128)(2,1)}, u32[]{:S(2)}, u32[]{:S(2)}) collective-permute-start(bf16[256,1024]{1,0:T(8,128)(2,1)} %select_convert_fusion), channel_id=1, source_target_pairs={{0,1},{1,0},{2,3},{3,2},{4,5},{5,4},{6,7},{7,6},{8,9},{9,8},{10,11... | collective-permute-start | bytes 1572872 | tf_op jit(solution)/shard_map/ppermute | solution.py:14
  208.3 25.2 %copy-start.1 = (bf16[256,2048]{1,0:T(8,128)(2,1)S(1)}, bf16[256,2048]{1,0:T(8,128)(2,1)}, u32[]{:S(2)}) copy-start(bf16[256,2048]{1,0:T(8,128)(2,1)} %param.6) | copy-start | bytes 3145732
  223.3 8.1 %copy-start.3 = (f32[256,2048]{1,0:T(8,128)S(1)}, f32[256,2048]{1,0:T(8,128)}, u32[]{:S(2)}) copy-start(f32[256,2048]{1,0:T(8,128)} %copy-done.2) | copy-start | bytes 6291460
